TPU v7x, 32 devices: a whole 2x2x4 slice. The times are simulated.
32 devices in a mesh: grp: 8 (over z, y), lag: 4 (over x, core).
Axes of the slice: x: 2, y: 2, z: 4, core: 2. Of those that a mesh axis runs over, the one named last changes fastest.
Arguments:
- history: float32 [8, 256, 32, 128], P('lag', 'grp'), may hold values from -6 to 6
- tiles: bfloat16 [16384, 128, 128], P(('grp', 'lag')), may hold values from -0.015625 to 0.015625
- tile_src: int32 [16384], P(('grp', 'lag')), may hold values from 0 to 255
- tile_obs: int32 [16384], P(('grp', 'lag')), may hold values from 0 to 16
- tile_lag: int32 [16384], P(('grp', 'lag')), may hold values from 0 to 1
- incident: float32 [16, 32, 128], P('grp', 'lag'), may hold values from -6 to 6
- near_inverse: bfloat16 [16, 128, 128], P('grp'), may hold values from -0.5 to 0.5
Outputs:
- field: float32 [16, 32, 128], P('grp', 'lag')
- new_current: float32 [16, 32, 128], P('grp', 'lag')
Inputs may be any that keep to these rules, and one draw needn't show every extreme that they name: `tile_obs`: a value of 16 marks a padded tile.
All inputs are finite; a program needn't handle non-finite values.
Results may differ from a plain program's by a relative error of at most 0.0035.
Values may be sent and summed in bfloat16 or wider, within the bound.
A program may use at most 128 MiB of HBM per device.

v0:
```python
import jax
import jax.numpy as jnp
from jax import lax
from jax.sharding import PartitionSpec as P

OBS_DEV = 2


def body(history, tiles, tile_src, tile_obs, tile_lag, incident, near_inverse):
    hist16 = history.astype(jnp.bfloat16)
    gathered = lax.all_gather(hist16, "grp", axis=1, tiled=True)
    lag_count = gathered.shape[0]
    source_count = gathered.shape[1]
    flat = gathered.reshape(lag_count * source_count, gathered.shape[2], gathered.shape[3])
    picked = flat[tile_lag * source_count + tile_src]
    terms = jnp.einsum("kas,kos->kao", picked, tiles, preferred_element_type=jnp.float32)
    observers = OBS_DEV * lax.axis_size("grp")
    partial_field = jax.ops.segment_sum(terms, tile_obs, num_segments=observers)
    angle_part = incident.shape[1]
    summed = lax.psum(partial_field, "lag")
    mine = lax.psum_scatter(summed, "grp", scatter_dimension=0, tiled=True)
    field = lax.dynamic_slice_in_dim(mine, lax.axis_index("lag") * angle_part, angle_part, 1)
    rhs = (incident - field).astype(jnp.bfloat16)
    new_current = jnp.einsum("oag,ohg->oah", rhs, near_inverse, preferred_element_type=jnp.float32)
    return (field, new_current)


def solution(mesh):
    return jax.shard_map(
        body,
        mesh=mesh,
        in_specs=(
            P("lag", "grp", None, None),
            P(("grp", "lag"), None, None),
            P(("grp", "lag")),
            P(("grp", "lag")),
            P(("grp", "lag")),
            P("grp", "lag", None),
            P("grp", None, None),
        ),
        out_specs=(P("grp", "lag", None), P("grp", "lag", None)),
        check_vma=False,
    )
```

profile of v0, /device:TPU:0, one launch (start us, length us, event | category | flops | bytes accessed | tf_op | source)
XLA Modules:
  0.0 230.3 jit_solution(4786745536430318728)
XLA Ops:
  7.2 0.0 copy-start
  7.2 0.0 all-gather.2.cloned.1.call-start
  7.2 2.1 convert_element_type.6
  9.3 0.0 all-gather.2.cloned.1.call-update
  9.4 0.0 reduce-scatter.2.cloned.1.call-start
  9.4 0.7 compare_select_fusion
  10.1 76.2 %all-gather.2.cloned.1.call-done = bf16[2,256,32,128]{3,2,1,0:T(8,128)(2,1)} async-done(((bf16[2,32,32,128]{3,2,1,0:T(8,128)(2,1)}), bf16[2,256,32,128]{3,2,1,0:T(8,128)(2,1)}) %all-gather.2.cloned.1.call-update) | async-done | bytes 4194320 | tf_op jit(solution)/shard_map/all_gather | solution.py:11
  86.3 5.4 %gather_fusion = bf16[512,32,128]{2,1,0:T(8,128)(2,1)} fusion(bf16[512,32,128]{2,1,0:T(8,128)(2,1)} %bitcast.4, s32[1024]{0:T(1024)S(1)} %pad_clamp_fusion), kind=kCustom, calls=%fused_computation | custom fusion | bytes 8390656 | tf_op jit(solution)/shard_map/gather | solution.py:15
  91.7 0.0 copy-start.4
  91.7 15.0 %fusion.1 = f32[512,32,128]{2,1,0:T(8,128)} fusion(bf16[512,32,128]{2,1,0:T(8,128)(2,1)} %gather_fusion, bf16[512,128,128]{2,1,0:T(8,128)(2,1)} %param.8), kind=kOutput, calls=%fused_computation.7 | convolution fusion | flops 536870912 | bytes 29360128 | tf_op jit(solution)/shard_map/kas,kos->kao/dot_general | solution.py:16
  106.7 0.0 copy-done.4
  106.7 0.0 copy-start.3
  106.7 44.9 %scatter_fusion = f32[16,32,128]{2,1,0:T(8,128)S(1)} fusion(f32[16,32,128]{2,1,0:T(8,128)S(1)} %broadcast_in_dim.9, s32[512]{0:T(512)S(1)} %copy-done.4, f32[512,32,128]{2,1,0:T(8,128)} %fusion.1), kind=kCustom, calls=%fused_computation.1 | custom fusion | flops 2097152 | bytes 25167872 | tf_op jit(solution)/shard_map/scatter-add | solution.py:18
  151.6 0.0 copy-start.1
  151.6 0.7 copy-done.1
  152.2 0.0 reduce-scatter.2.cloned.1.call-update
  152.3 59.6 %reduce-scatter.2.cloned.1.call-done = f32[2,32,128]{2,1,0:T(8,128)} async-done(((f32[16,32,128]{2,1,0:T(8,128)}), f32[2,32,128]{2,1,0:T(8,128)}) %reduce-scatter.2.cloned.1.call-update) | async-done | bytes 32784 | tf_op jit(solution)/shard_map/reduce_scatter | solution.py:21
  211.9 10.8 %psum.8 = f32[2,32,128]{2,1,0:T(8,128)S(1)} all-reduce(f32[2,32,128]{2,1,0:T(8,128)} %reduce-scatter.2.cloned.1.call-done), channel_id=1, replica_groups=mesh['grp'=8,'lag'=4] {'lag'}, use_global_device_ids=true, to_apply=%region_1.0 | all-reduce | flops 8192 | bytes 65536 | tf_op jit(solution)/shard_map/psum | solution.py:20
  222.7 0.0 copy-done
  222.7 0.0 copy-done.3
  222.7 0.0 copy-start.2
  222.7 0.7 fusion
  223.5 0.0 copy-done.2
  (3 shorter events, 0.0 us)
Async XLA Ops:
  7.2 215.5 %copy-start = (bf16[2,128,128]{2,1,0:T(8,128)(2,1)S(1)}, bf16[2,128,128]{2,1,0:T(8,128)(2,1)}, u32[]{:S(2)}) copy-start(bf16[2,128,128]{2,1,0:T(8,128)(2,1)} %param.13) | copy-start | bytes 196612
  7.2 79.1 %all-gather.2.cloned.1.call-start = ((), (), s32[]{:S(2)}) async-start(), calls=%async_computation.1 | async-start | bytes 4718592 | tf_op jit(solution)/shard_map/all_gather | solution.py:11
  9.4 202.5 %reduce-scatter.2.cloned.1.call-start = ((), (), s32[]{:S(2)}) async-start(), calls=%async_computation.2 | async-start | bytes 294912 | tf_op jit(solution)/shard_map/reduce_scatter | solution.py:21
  91.7 15.0 %copy-start.4 = (s32[512]{0:T(512)S(1)}, s32[512]{0:T(512)}, u32[]{:S(2)}) copy-start(s32[512]{0:T(512)} %param.10) | copy-start | bytes 6148
  106.7 116.0 %copy-start.3 = (f32[2,8,128]{2,1,0:T(8,128)S(1)}, f32[2,8,128]{2,1,0:T(8,128)}, u32[]{:S(2)}) copy-start(f32[2,8,128]{2,1,0:T(8,128)} %param.12) | copy-start | bytes 24580
  151.6 0.7 copy-start.1
  222.7 0.8 copy-start.2
Sparse Core Ops, SparseCore 0:
  10.2 76.0 all-gather.1
  152.4 59.4 reduce-scatter.1
where the time goes:
time: 232 us; the launch traced here: 230 us
  waiting for transfers between devices  136 us (59%)
  other arithmetic  47.7 us (21%)
  matrix products  15.7 us (7%)
  between operations  14.1 us (6%)
  blocking collectives  10.8 us (5%)
  local copies, waits for them, and re-layouts  6.09 us (3%)
    all_gather x1, waiting for transfers between devices, body(): gathered = lax.all_gather(hist16, 'grp', axis=1, tiled=True)  76.2 us
    reduce_scatter x1, waiting for transfers between devices, body(): mine = lax.psum_scatter(summed, 'grp', scatter_dimension=0, tiled=True)  59.6 us
    scatter-add x1, other arithmetic, body(): partial_field = jax.ops.segment_sum(terms, tile_obs, num_segments=observers)  44.9 us
    dot_general x1, matrix products, body(): jnp.einsum('kas,kos->kao', picked, tiles, preferred_element_type=jnp.floa...  15 us
    psum x1, blocking collectives, body(): summed = lax.psum(partial_field, 'lag')  10.8 us
    gather x1, local copies, waits for them, and re-layouts, body(): picked = flat[tile_lag * source_count + tile_src]  5.35 us
  transfers between devices with their start and end apart: 2, of which 2 were waited for; matrix products, arithmetic and copies ran while one was open for 0% of the time, Pallas kernels for 0%

commit v1 on v0

v1 whole, which is shorter than its diff:
```python
import functools

import jax
import jax.numpy as jnp
from jax import lax
from jax.experimental import pallas as pl
from jax.experimental.pallas import tpu as pltpu
from jax.sharding import PartitionSpec as P

MIB = 1 << 20


def gather_kernel(n_slow, n_fast, chunks, early, hist_ref, out_ref, own, send_sem, recv_sem, local_sem):
    lags, per_dev = own.shape[0], own.shape[1]
    per_lag = chunks // lags
    size = per_dev // per_lag
    me = lax.axis_index("grp")
    z, y = me // n_fast, me % n_fast

    def place(column, c):
        return c // per_lag, (c % per_lag) * size

    def home(origin, c):
        lag, start = place(origin, c)
        return out_ref.at[lag, pl.ds(origin * per_dev + start, size)]

    def mine(c):
        lag, start = place(me, c)
        return own.at[lag, pl.ds(start, size)]

    def remote(src, origin, c, slot, target):
        return pltpu.make_async_remote_copy(
            src_ref=src,
            dst_ref=home(origin, c),
            send_sem=send_sem.at[origin, c, slot],
            recv_sem=recv_sem.at[origin, c],
            device_id={"grp": target},
            device_id_type=pl.DeviceIdType.MESH,
        )

    def wait_arrival(origin, c):
        remote(home(origin, c), origin, c, 0, me).wait_recv()

    def along(step, origin, c, src, drain):
        @pl.when((z + step >= 0) & (z + step < n_slow))
        def _():
            copy = remote(src, origin, c, 0 if step < 0 else 1, me + step * n_fast)
            copy.wait_send() if drain else copy.start()

    def across(origin, c, src, drain):
        for j in range(1, n_fast):
            copy = remote(src, origin, c, 1 + j, z * n_fast + (y + j) % n_fast)
            copy.wait_send() if drain else copy.start()

    def walk(drain):
        @pl.loop(0, chunks)
        def _(c):
            across(me, c, mine(c), drain)
            along(-1, me, c, mine(c), drain)
            along(1, me, c, mine(c), drain)

        for j in range(1, n_fast):
            peer = z * n_fast + (y + j) % n_fast
            for c in range(early):
                if not drain:
                    wait_arrival(peer, c)
                along(-1, peer, c, home(peer, c), drain)
                along(1, peer, c, home(peer, c), drain)

        for d in range(1, n_slow):

            @pl.loop(0, chunks)
            def _(c):
                for sign in (1, -1):

                    @pl.when((z + sign * d >= 0) & (z + sign * d < n_slow))
                    def _():
                        origin = me + sign * d * n_fast
                        if not drain:
                            wait_arrival(origin, c)
                        along(-sign, origin, c, home(origin, c), drain)

                        @pl.when(c >= early)
                        def _():
                            across(origin, c, home(origin, c), drain)

            for j in range(1, n_fast):
                for c in range(early):
                    for sign in (1, -1):

                        @pl.when((z + sign * d >= 0) & (z + sign * d < n_slow))
                        def _():
                            origin = (z + sign * d) * n_fast + (y + j) % n_fast
                            if not drain:
                                wait_arrival(origin, c)
                            along(-sign, origin, c, home(origin, c), drain)

    barrier = pltpu.get_barrier_semaphore()
    for step in (-1, 1):

        @pl.when((z + step >= 0) & (z + step < n_slow))
        def _():
            pl.semaphore_signal(
                barrier, inc=1, device_id={"grp": me + step * n_fast}, device_id_type=pl.DeviceIdType.MESH
            )

    for j in range(1, n_fast):
        pl.semaphore_signal(
            barrier, inc=1, device_id={"grp": z * n_fast + (y + j) % n_fast}, device_id_type=pl.DeviceIdType.MESH
        )
    own[...] = hist_ref[...].astype(own.dtype)
    pl.semaphore_wait(barrier, jnp.where(z > 0, 1, 0) + jnp.where(z < n_slow - 1, 1, 0) + n_fast - 1)

    kept = pltpu.make_async_copy(own, out_ref.at[:, pl.ds(me * per_dev, per_dev)], local_sem)
    kept.start()
    walk(False)
    for j in range(1, n_fast):
        column = (y + j) % n_fast
        for d in range(n_slow):
            origin = (z + d) % n_slow * n_fast + column

            @pl.loop(early, chunks)
            def _(c):
                wait_arrival(origin, c)

    kept.wait()
    walk(True)


def gather(history, n_grp):
    lags, per_dev, angles, width = history.shape
    n_slow = 4 if n_grp % 4 == 0 else 1
    n_fast = n_grp // n_slow
    chunks = lags * 4
    return pl.pallas_call(
        functools.partial(gather_kernel, n_slow, n_fast, chunks, 1),
        out_shape=jax.ShapeDtypeStruct((lags, n_grp * per_dev, angles, width), jnp.bfloat16),
        in_specs=[pl.BlockSpec(memory_space=pltpu.VMEM)],
        out_specs=pl.BlockSpec(memory_space=pl.ANY),
        scratch_shapes=[
            pltpu.VMEM(history.shape, jnp.bfloat16),
            pltpu.SemaphoreType.DMA((n_grp, chunks, 1 + n_fast)),
            pltpu.SemaphoreType.DMA((n_grp, chunks)),
            pltpu.SemaphoreType.DMA,
        ],
        compiler_params=pltpu.CompilerParams(collective_id=0, has_side_effects=True, vmem_limit_bytes=16 * MIB),
        name="gather",
    )(history)


def products_kernel(sources, unroll, src_ref, obs_ref, lag_ref, hist_ref, tiles_ref, out_ref, acc):
    block = tiles_ref.shape[0]
    step = pl.program_id(0)
    copies = acc.shape[0]
    observers = out_ref.shape[1]
    part = out_ref.shape[2]

    @pl.when(step == 0)
    def _():
        acc[...] = jnp.zeros_like(acc)

    @pl.loop(0, block // unroll)
    def _(i):
        for u in range(unroll):
            local = i * unroll + u
            r = step * block + local
            picked = hist_ref[lag_ref[r] * sources + src_ref[r]]
            term = lax.dot_general(
                picked, tiles_ref[local], (((1,), (1,)), ((), ())), preferred_element_type=jnp.float32
            )
            acc[u % copies, obs_ref[r]] += term

    @pl.when(step == pl.num_programs(0) - 1)
    def _():
        total = acc[0, :observers]
        for k in range(1, copies):
            total = total + acc[k, :observers]
        for j in range(out_ref.shape[0]):
            out_ref[j] = total[:, j * part : (j + 1) * part]


def products(gathered, tiles, tile_src, tile_obs, tile_lag, observers, n_lag):
    lags, sources, angles, width = gathered.shape
    count = tiles.shape[0]
    block = 64
    out = (n_lag, observers, angles // n_lag, width)
    return pl.pallas_call(
        functools.partial(products_kernel, sources, 16),
        out_shape=jax.ShapeDtypeStruct(out, jnp.float32),
        grid=(count // block,),
        in_specs=[pl.BlockSpec(memory_space=pltpu.SMEM)] * 3
        + [
            pl.BlockSpec((lags * sources, angles, width), lambda i: (0, 0, 0)),
            pl.BlockSpec((block, width, width), lambda i: (i, 0, 0)),
        ],
        out_specs=pl.BlockSpec(out, lambda i: (0, 0, 0, 0)),
        scratch_shapes=[pltpu.VMEM((4, observers + 1, angles, width), jnp.float32)],
        compiler_params=pltpu.CompilerParams(vmem_limit_bytes=48 * MIB),
        name="products",
    )(tile_src, tile_obs, tile_lag, gathered.reshape(lags * sources, angles, width), tiles)


def finish_kernel(
    n_grp, n_lag, partial_ref, incident_ref, near_ref, field_ref, current_ref, by_lag, summed, by_grp, send1, recv1, send2, recv2
):
    g, l = lax.axis_index("grp"), lax.axis_index("lag")
    mine = field_ref.shape[0]
    barrier = pltpu.get_barrier_semaphore()
    for axis, me, n in (("lag", l, n_lag), ("grp", g, n_grp)):
        for j in range(1, n):
            pl.semaphore_signal(
                barrier, inc=1, device_id={axis: (me + j) % n}, device_id_type=pl.DeviceIdType.MESH
            )
    pl.semaphore_wait(barrier, n_lag + n_grp - 2)

    copies = []
    for j in range(1, n_lag):
        target = (l + j) % n_lag
        copy = pltpu.make_async_remote_copy(
            src_ref=partial_ref.at[target],
            dst_ref=by_lag.at[j - 1],
            send_sem=send1.at[j - 1],
            recv_sem=recv1.at[j - 1],
            device_id={"lag": target},
            device_id_type=pl.DeviceIdType.MESH,
        )
        copy.start()
        copies.append(copy)
    total = partial_ref[l]
    for j, copy in enumerate(copies):
        copy.wait_recv()
        total = total + by_lag[j]
    summed[...] = total

    later = []
    for j in range(1, n_grp):
        target = (g + j) % n_grp
        copy = pltpu.make_async_remote_copy(
            src_ref=summed.at[pl.ds(target * mine, mine)],
            dst_ref=by_grp.at[j - 1],
            send_sem=send2.at[j - 1],
            recv_sem=recv2.at[j - 1],
            device_id={"grp": target},
            device_id_type=pl.DeviceIdType.MESH,
        )
        copy.start()
        later.append(copy)
    field = summed[pl.ds(g * mine, mine)]
    for j, copy in enumerate(later):
        copy.wait_recv()
        field = field + by_grp[j]
    field_ref[...] = field
    rhs = (incident_ref[...] - field).astype(jnp.bfloat16)
    for o in range(mine):
        current_ref[o] = lax.dot_general(
            rhs[o], near_ref[o], (((1,), (1,)), ((), ())), preferred_element_type=jnp.float32
        )
    for copy in copies + later:
        copy.wait_send()


def finish(partial, incident, near_inverse, n_grp):
    n_lag, observers, part, width = partial.shape
    shape = jax.ShapeDtypeStruct(incident.shape, jnp.float32)
    return pl.pallas_call(
        functools.partial(finish_kernel, n_grp, n_lag),
        out_shape=(shape, shape),
        in_specs=[pl.BlockSpec(memory_space=pltpu.VMEM)] * 3,
        out_specs=(pl.BlockSpec(memory_space=pltpu.VMEM),) * 2,
        scratch_shapes=[
            pltpu.VMEM((n_lag - 1, observers, part, width), jnp.float32),
            pltpu.VMEM((observers, part, width), jnp.float32),
            pltpu.VMEM((n_grp - 1,) + incident.shape, jnp.float32),
            pltpu.SemaphoreType.DMA((n_lag - 1,)),
            pltpu.SemaphoreType.DMA((n_lag - 1,)),
            pltpu.SemaphoreType.DMA((n_grp - 1,)),
            pltpu.SemaphoreType.DMA((n_grp - 1,)),
        ],
        compiler_params=pltpu.CompilerParams(collective_id=1, has_side_effects=True, vmem_limit_bytes=16 * MIB),
        name="finish",
    )(partial, incident, near_inverse)


def body(history, tiles, tile_src, tile_obs, tile_lag, incident, near_inverse):
    n_grp, n_lag = lax.axis_size("grp"), lax.axis_size("lag")
    observers = incident.shape[0] * n_grp
    gathered = gather(history, n_grp)
    partial = products(gathered, tiles, tile_src, tile_obs, tile_lag, observers, n_lag)
    return finish(partial, incident, near_inverse, n_grp)


def solution(mesh):
    return jax.shard_map(
        body,
        mesh=mesh,
        in_specs=(
            P("lag", "grp", None, None),
            P(("grp", "lag"), None, None),
            P(("grp", "lag")),
            P(("grp", "lag")),
            P(("grp", "lag")),
            P("grp", "lag", None),
            P("grp", None, None),
        ),
        out_specs=(P("grp", "lag", None), P("grp", "lag", None)),
        check_vma=False,
    )
```

time: 232 us -> 79.5 us (0.34)
  waiting for transfers between devices: 136 us -> 0 us
  Pallas kernels: 0 us -> 73.9 us
  other arithmetic: 47.7 us -> 0 us
  matrix products: 15.7 us -> 0 us
  between operations: 14.1 us -> 0.69 us
  blocking collectives: 10.8 us -> 0 us
    all_gather x1 -> x0, waiting for transfers between devices: 76.2 us -> none  [body(): gathered = lax.all_gather(hist16, 'grp', axis=1, tiled=True)]
    pallas_call x0 -> x3, Pallas kernels: none -> 73.9 us  [the longest x1 48.8 us: gather(): pl.pallas_call(functools.partial(gather_kernel, n_slow, n_fast, chunks, 1...]
    reduce_scatter x1 -> x0, waiting for transfers between devices: 59.6 us -> none  [body(): mine = lax.psum_scatter(summed, 'grp', scatter_dimension=0, tiled=True)]
    scatter-add x1 -> x0, other arithmetic: 44.9 us -> none  [body(): partial_field = jax.ops.segment_sum(terms, tile_obs, num_segments=observers)]
    dot_general x2 -> x0, matrix products: 15.7 us -> none  [the longest x1 15 us: body(): jnp.einsum('kas,kos->kao', picked, tiles, preferred_element_type=jnp.floa...]
    psum x1 -> x0, blocking collectives: 10.8 us -> none  [body(): summed = lax.psum(partial_field, 'lag')]
    gather x1 -> x0, local copies, waits for them, and re-layouts: 5.35 us -> none  [body(): picked = flat[tile_lag * source_count + tile_src]]
    unnamed x10 -> x14, local copies, waits for them, and re-layouts: 0.71 us -> 4.46 us
  transfers between devices with their start and end apart: 2 -> 0, of which waited for: 2 -> 0; matrix products, arithmetic and copies ran while one was open for 0% -> 0% of each run, Pallas kernels for 0% -> 0%
where the time goes in v1:
time: 79.5 us; the launch traced here: 79.1 us
  Pallas kernels  73.9 us (93%)
  local copies, waits for them, and re-layouts  4.46 us (6%)
    pallas_call x1, Pallas kernels, gather(): pl.pallas_call(functools.partial(gather_kernel, n_slow, n_fast, chunks, 1...  48.8 us
    pallas_call x1, Pallas kernels, products(): pl.pallas_call(functools.partial(products_kernel, sources, 16), out_shape...  14.5 us
    pallas_call x1, Pallas kernels, finish(): pl.pallas_call(functools.partial(finish_kernel, n_grp, n_lag), out_shape=...  10.7 us
    unnamed x14, local copies, waits for them, and re-layouts  4.46 us

profile of v1, /device:TPU:0, one launch (start us, length us, event | category | flops | bytes accessed | tf_op | source)
XLA Modules:
  0.0 79.1 jit_solution(13531171977045689318)
XLA Ops:
  0.6 0.0 copy-start
  0.6 1.2 %copy-done = f32[2,32,32,128]{3,2,1,0:T(8,128)S(1)} copy-done((f32[2,32,32,128]{3,2,1,0:T(8,128)S(1)}, f32[2,32,32,128]{3,2,1,0:T(8,128)}, u32[]{:S(2)}) %copy-start) | copy-done | bytes 1048600
  1.9 0.0 copy-start.1
  1.9 0.0 copy-start.2
  1.9 48.8 %gather.1 = bf16[2,256,32,128]{3,2,1,0:T(8,128)(2,1)S(1)} custom-call(f32[2,32,32,128]{3,2,1,0:T(8,128)S(1)} %copy-done), custom_call_target="tpu_custom_call" | custom-call | tf_op jit(solution)/shard_map/gather/pallas_call | solution.py:135
  50.7 0.0 copy-start.3
  50.7 0.7 copy-done.3
  51.4 0.0 copy-start.4
  51.4 0.7 copy-done.4
  52.1 0.0 copy-start.5
  52.1 0.7 copy-done.5
  52.8 14.5 %products.1.partial_ref = f32[4,16,8,128]{3,2,1,0:T(8,128)S(1)} custom-call(s32[512]{0:T(512)S(1)} %copy-done.3, s32[512]{0:T(512)S(1)} %copy-done.4, s32[512]{0:T(512)S(1)} %copy-done.5, bf16[512,32,128]{2,1,0:T(8,128)(2,1)S(1)} %bitcast.1, bf16[512,128,128]{2,1,0:T(8,128)(2,1)} %tiles_ref.1), custom_call_target="tpu_custom_call" | custom-call | tf_op jit(solution)/shard_map/products/pallas_call | solution.py:187
  67.2 0.0 copy-done.1
  67.2 0.0 copy-done.2
  67.2 10.7 %finish.1 = (f32[2,8,128]{2,1,0:T(8,128)S(1)}, f32[2,8,128]{2,1,0:T(8,128)S(1)}) custom-call(f32[4,16,8,128]{3,2,1,0:T(8,128)S(1)} %products.1.partial_ref, f32[2,8,128]{2,1,0:T(8,128)S(1)} %copy-done.2, bf16[2,128,128]{2,1,0:T(8,128)(2,1)S(1)} %copy-done.1), custom_call_target="tpu_custom_call" | custom-call | tf_op jit(solution)/shard_map/finish/pallas_call | solution.py:265
  77.9 0.6 copy.11
  78.5 0.6 copy.12
Async XLA Ops:
  0.6 1.2 %copy-start = (f32[2,32,32,128]{3,2,1,0:T(8,128)S(1)}, f32[2,32,32,128]{3,2,1,0:T(8,128)}, u32[]{:S(2)}) copy-start(f32[2,32,32,128]{3,2,1,0:T(8,128)} %hist_ref.1) | copy-start | bytes 3145732
  1.9 65.4 %copy-start.1 = (bf16[2,128,128]{2,1,0:T(8,128)(2,1)S(1)}, bf16[2,128,128]{2,1,0:T(8,128)(2,1)}, u32[]{:S(2)}) copy-start(bf16[2,128,128]{2,1,0:T(8,128)(2,1)} %near_ref.1) | copy-start | bytes 196612
  1.9 65.4 %copy-start.2 = (f32[2,8,128]{2,1,0:T(8,128)S(1)}, f32[2,8,128]{2,1,0:T(8,128)}, u32[]{:S(2)}) copy-start(f32[2,8,128]{2,1,0:T(8,128)} %incident_ref.1) | copy-start | bytes 24580
  50.7 0.7 copy-start.3
  51.4 0.7 copy-start.4
  52.1 0.7 copy-start.5
